TPU v7x, 512 devices: a whole 4x4x16 slice. The times are simulated.
512 devices in a mesh: rows: 64 (over x, z), cols: 8 (over y, core).
Axes of the slice: x: 4, y: 4, z: 16, core: 2. Of those that a mesh axis runs over, the one named last changes fastest.
Arguments:
- right_side: float32 [16, 32768], P(None, 'rows'), may hold values from -6 to 6
- child_updates: float32 [16384, 16, 128], P('rows', 'cols'), may hold values from -6 to 6
- child_device: int32 [16384, 1], P('rows'), may hold values from 0 to 63; in each aligned block of 256 rows (0 to 255, 256 to 511, ...) at most 8 rows name the same one
- child_block: int32 [16384, 1], P('rows'), may hold values from 0 to 3
- owners: int32 [2], replicated, may hold values from 0 to 63, as said below
- diag_inverse: bfloat16 [2, 512, 512], P(None, 'cols'), may hold values from -0.25 to 0.25
- panel_factor: bfloat16 [2, 512, 32768], P(None, 'cols', 'rows'), may hold values from -0.25 to 0.25
Outputs:
- front_state: float32 [16, 32768], P(None, 'rows')
Inputs may be any that keep to these rules, and one draw needn't show every extreme that they name: `child_device`: among the child blocks of one rows index (aligned blocks of 256 rows) no panel is named more than 8 times. `owners`: the entries are distinct.
All inputs are finite; a program needn't handle non-finite values.
Results may differ from a plain program's by a relative error of at most 0.0003.
Values sent between devices are 32-bit elements; how exact they have to be, the bound alone decides.
A program may use at most 64 MiB of HBM per device.

v0:
```python
import jax
import jax.numpy as jnp
from jax import lax
from jax.sharding import PartitionSpec as P


def broadcast(shard, axis, root):
    mine = lax.axis_index(axis) == root
    return lax.psum(jnp.where(mine, shard, jnp.zeros_like(shard)), axis)


def body(right_side, child_updates, child_device, child_block, owners, diag_inverse, panel_factor):
    nrows = lax.axis_size("rows")
    count_blocks, kc, blk = child_updates.shape
    panel = right_side.shape[1]
    per_panel = panel // blk
    capacity = max(2, 2 * count_blocks // nrows)
    target = child_device[:, 0]
    hits = (target[:, None] == jnp.arange(nrows, dtype=jnp.int32)[None, :]).astype(jnp.int32)
    before = jnp.cumsum(hits, axis=0) - hits
    slot = jnp.sum(before * hits, axis=1)
    places = target * capacity + slot
    send_vals = jnp.zeros((nrows * capacity, kc, blk), jnp.float32).at[places].set(child_updates)
    send_vals = send_vals.reshape(nrows, capacity, kc, blk)
    send_tags = (
        jnp.full((nrows * capacity,), -1.0, jnp.float32)
        .at[places]
        .set(child_block[:, 0].astype(jnp.float32))
    )
    send_tags = send_tags.reshape(nrows, capacity)
    recv_vals, recv_tags = (
        lax.all_to_all(send_vals, "rows", split_axis=0, concat_axis=0, tiled=True),
        lax.all_to_all(send_tags, "rows", split_axis=0, concat_axis=0, tiled=True),
    )
    select = (
        recv_tags.reshape(-1)[:, None] == jnp.arange(per_panel, dtype=jnp.float32)[None, :]
    ).astype(jnp.float32)
    assembled = jnp.einsum(
        "sb,skc->kbc", select, recv_vals.reshape(-1, kc, blk), precision=lax.Precision.HIGHEST
    )
    assembled = assembled.reshape(kc, panel)
    full_cols = lax.all_gather(assembled, "cols", axis=0, tiled=True)
    state = right_side + full_cols
    myself = lax.axis_index("rows")
    for step in range(owners.shape[0]):
        root = owners[step]
        side = broadcast(state, "rows", root)
        part_solution = jnp.dot(
            side, diag_inverse[step].astype(jnp.float32).T, precision=lax.Precision.HIGHEST
        )
        partial_value = jnp.dot(
            part_solution, panel_factor[step].astype(jnp.float32), precision=lax.Precision.HIGHEST
        )
        update = lax.psum(partial_value, "cols")
        solved = lax.all_gather(part_solution, "cols", axis=1, tiled=True)
        finished = jnp.any(owners[: step + 1] == myself)
        state = jnp.where(myself == root, solved, jnp.where(finished, state, state - update))
    return state


def solution(mesh):
    return jax.shard_map(
        body,
        mesh=mesh,
        in_specs=(
            P(None, "rows"),
            P("rows", "cols", None),
            P("rows", None),
            P("rows", None),
            P(),
            P(None, "cols", None),
            P(None, "cols", "rows"),
        ),
        out_specs=P(None, "rows"),
        check_vma=False,
    )
```

profile of v0, /device:TPU:1, one launch (start us, length us, event | category | flops | bytes accessed | tf_op | source)
XLA Modules:
  0.0 717.2 jit_solution(1559028892850668551)
XLA Ops:
  0.0 0.7 copy-done.4
  0.7 0.6 reduce-window.6
  1.3 0.2 slice_reduce_fusion
  1.5 0.1 fusion.4
  1.7 0.7 copy-done.6
  2.3 1.4 scatter_custom_fusion.1
  3.7 0.7 all_to_all.10
  4.4 19.1 %all-to-all-start.1 = ((f32[64,1,8]{2,1,0:T(1,128)}), f32[64,1,8]{2,1,0:T(1,128)S(1)}, u32[]{:S(2)}, u32[]{:S(2)}) async-start(f32[64,1,8]{2,1,0:T(1,128)} %bitcast.10), calls=%async_computation.1 | async-start | bytes 65536 | tf_op jit(solution)/shard_map/all_to_all | solution.py:33
  23.6 0.1 broadcast_in_dim.4
  23.7 0.8 copy-done
  24.5 7.0 scatter_fusion
  31.5 0.8 copy.14
  32.3 4.5 all-to-all-done.1
  36.8 10.1 %all-to-all-start = ((f32[64,8,2,128]{3,1,2,0:T(8,128)}), f32[64,8,2,128]{3,1,2,0:T(8,128)S(1)}, u32[]{:S(2)}, u32[]{:S(2)}) async-start(f32[64,8,2,128]{3,1,2,0:T(8,128)} %copy.14), calls=%async_computation | async-start | bytes 1048576 | tf_op jit(solution)/shard_map/all_to_all | solution.py:32
  46.9 0.6 copy-done.5
  47.5 0.6 fusion.26
  50.0 0.6 compare_reduce_fusion
  50.6 0.5 broadcast.41
  51.1 0.7 reduce.5
  51.9 23.8 %all-to-all-done = f32[64,8,2,128]{3,1,2,0:T(8,128)S(1)} async-done(((f32[64,8,2,128]{3,1,2,0:T(8,128)}), f32[64,8,2,128]{3,1,2,0:T(8,128)S(1)}, u32[]{:S(2)}, u32[]{:S(2)}) %all-to-all-start) | async-done | bytes 524320 | tf_op jit(solution)/shard_map/all_to_all | solution.py:32
  75.8 0.2 convolution_bitcast_fusion
  76.1 16.4 %all-gather = f32[8,2,512]{2,1,0:T(2,128)S(1)} all-gather(f32[1,2,512]{2,1,0:T(2,128)S(1)} %reshape.54), channel_id=1, replica_groups=mesh['rows'=64,'cols'=8] {'cols'}, dimensions={0}, use_global_device_ids=true | all-gather | bytes 36864 | tf_op jit(solution)/shard_map/all_gather | solution.py:42
  92.6 221.5 %psum.28 = f32[16,512]{1,0:T(8,128)S(1)} all-reduce(f32[16,512]{1,0:T(8,128)S(1)} %get-tuple-element.7), channel_id=1, replica_groups=mesh['rows'=64,'cols'=8] {'rows'}, use_global_device_ids=true, to_apply=%region_5.6 | all-reduce | flops 8192 | bytes 65536 | tf_op jit(solution)/shard_map/psum | solution.py:9
  314.1 67.5 %all-gather.1 = f32[8,64,16]{1,2,0:T(8,128)S(1)} all-gather(f32[1,64,16]{1,2,0:T(8,128)S(1)} %bitcast.70), channel_id=1, replica_groups=mesh['rows'=64,'cols'=8] {'cols'}, dimensions={0}, use_global_device_ids=true | all-gather | bytes 36864 | tf_op jit(solution)/shard_map/all_gather | solution.py:55
  381.8 0.8 copy-done.2
  382.6 0.1 fusion.9
  382.7 22.5 %psum.29 = f32[16,512]{1,0:T(8,128)S(1)} all-reduce(f32[16,512]{1,0:T(8,128)S(1)} %fusion.9), channel_id=1, replica_groups=mesh['rows'=64,'cols'=8] {'cols'}, use_global_device_ids=true, to_apply=%region_6.7 | all-reduce | flops 8192 | bytes 65536 | tf_op jit(solution)/shard_map/psum | solution.py:54
  405.2 219.4 %psum.30 = f32[16,512]{1,0:T(8,128)S(1)} all-reduce(f32[16,512]{1,0:T(8,128)S(1)} %get-tuple-element.5), channel_id=1, replica_groups=mesh['rows'=64,'cols'=8] {'rows'}, use_global_device_ids=true, to_apply=%region_7.8 | all-reduce | flops 8192 | bytes 65536 | tf_op jit(solution)/shard_map/psum | solution.py:9
  624.7 0.2 fusion.5
  624.9 70.7 %all-gather.2 = f32[8,64,16]{1,2,0:T(8,128)S(1)} all-gather(f32[1,64,16]{1,2,0:T(8,128)S(1)} %bitcast.71), channel_id=1, replica_groups=mesh['rows'=64,'cols'=8] {'cols'}, dimensions={0}, use_global_device_ids=true | all-gather | bytes 36864 | tf_op jit(solution)/shard_map/all_gather | solution.py:55
  695.7 20.4 %psum.31 = f32[16,512]{1,0:T(8,128)S(1)} all-reduce(f32[16,512]{1,0:T(8,128)S(1)} %fusion.5), channel_id=1, replica_groups=mesh['rows'=64,'cols'=8] {'cols'}, use_global_device_ids=true, to_apply=%region_9.10 | all-reduce | flops 8192 | bytes 65536 | tf_op jit(solution)/shard_map/psum | solution.py:54
  716.1 1.2 fusion.19
  (25 shorter events, 0.7 us)
Async XLA Ops:
  0.0 0.7 copy-start.4
  1.6 0.7 copy-start.6
  4.4 32.3 %all-to-all-start.1 = ((f32[64,1,8]{2,1,0:T(1,128)}), f32[64,1,8]{2,1,0:T(1,128)S(1)}, u32[]{:S(2)}, u32[]{:S(2)}) async-start(f32[64,1,8]{2,1,0:T(1,128)} %bitcast.10), calls=%async_computation.1 | async-start | bytes 65536 | tf_op jit(solution)/shard_map/all_to_all | solution.py:33
  23.6 1.0 copy-start
  36.8 39.0 %all-to-all-start = ((f32[64,8,2,128]{3,1,2,0:T(8,128)}), f32[64,8,2,128]{3,1,2,0:T(8,128)S(1)}, u32[]{:S(2)}, u32[]{:S(2)}) async-start(f32[64,8,2,128]{3,1,2,0:T(8,128)} %copy.14), calls=%async_computation | async-start | bytes 1048576 | tf_op jit(solution)/shard_map/all_to_all | solution.py:32
  46.9 0.7 copy-start.5
  75.8 16.8 %copy-start.3 = (f32[16,512]{1,0:T(8,128)S(1)}, f32[16,512]{1,0:T(8,128)}, u32[]{:S(2)}) copy-start(f32[16,512]{1,0:T(8,128)} %param.7) | copy-start | bytes 98308
  92.5 221.5 %copy-start.1 = (bf16[2,64,512]{2,1,0:T(8,128)(2,1)S(1)}, bf16[2,64,512]{2,1,0:T(8,128)(2,1)}, u32[]{:S(2)}) copy-start(bf16[2,64,512]{2,1,0:T(8,128)(2,1)} %param.12) | copy-start | bytes 393220
  381.7 0.9 copy-start.2
where the time goes:
time: 718 us; the launch traced here: 717 us
  blocking collectives  638 us (89%)
  starting transfers between devices  29.2 us (4%)
  waiting for transfers between devices  28.3 us (4%)
  local copies, waits for them, and re-layouts  15.3 us (2%)
    psum x2, blocking collectives, broadcast(): return lax.psum(jnp.where(mine, shard, jnp.zeros_like(shard)), axis)  441 us
    all_gather x2, blocking collectives, body(): solved = lax.all_gather(part_solution, 'cols', axis=1, tiled=True)  138 us
    psum x2, blocking collectives, body(): update = lax.psum(partial_value, 'cols')  42.9 us
    all_to_all x1, waiting for transfers between devices, body(): lax.all_to_all(send_vals, 'rows', split_axis=0, concat_axis=0, tiled=True)  23.8 us
    all_to_all x1, starting transfers between devices, body(): lax.all_to_all(send_tags, 'rows', split_axis=0, concat_axis=0, tiled=True)  19.1 us
    all_gather x1, blocking collectives, body(): full_cols = lax.all_gather(assembled, 'cols', axis=0, tiled=True)  16.4 us
  transfers between devices with their start and end apart: 2, of which 2 were waited for; matrix products, arithmetic and copies ran while one was open for 1% of the time, Pallas kernels for 0%

commit v1 on v0

v1 whole, which is shorter than its diff:
```python
import functools

import jax
import jax.numpy as jnp
from jax import lax
from jax.experimental import pallas as pl
from jax.experimental.pallas import tpu as pltpu
from jax.sharding import PartitionSpec as P

MESH = pl.DeviceIdType.MESH
F32, BF16 = jnp.float32, jnp.bfloat16
NX, NY, NC, NZ = 4, 4, 2, 16

Z_OFFS = (8, 7, 9, 6, 10, 5, 11, 4, 12, 3, 13, 2, 14, 1, 15)
X_OFFS = (2, 1, 3)
C_OFFS = tuple((dy, dk) for dy in (2, 1, 3, 0) for dk in (0, 1) if dy or dk)
XC_OFFS = tuple((dx, dy, dk) for dx in (2, 1, 3, 0) for dy in (2, 1, 3, 0) for dk in (0, 1) if dx or dy or dk)


def split(value):
    high = value.astype(BF16)
    return high, (value - high.astype(F32)).astype(BF16)


def stacked(value):
    return jnp.concatenate(split(value), axis=0)


def folded(value):
    half = value.shape[0] // 2
    return value[:half] + value[half:]


def dot(a, b):
    return jnp.dot(a, b, preferred_element_type=F32)


def dot_t(a, b):
    return lax.dot_general(a, b, (((1,), (1,)), ((), ())), preferred_element_type=F32)


def kernel(
    owners, right, child, dev, blk, diag, fac, out,
    summed, fmask, fz, fmine, fx, pown, pz, pmine, px, dmine, dg, mx, mmine, mz, tz, part, pr, xs, rown, order, send, recv,
):
    row, col = lax.axis_index("rows"), lax.axis_index("cols")
    x, z, y, k = row // NZ, row % NZ, col // NC, col % NC

    def z_peer(d):
        return (x * NZ + (z + d) % NZ, col)

    def x_peer(d):
        return ((x + d) % NX * NZ + z, col)

    def c_peer(d):
        return (row, (y + d[0]) % NY * NC + (k + d[1]) % NC)

    def xc_peer(d):
        return ((x + d[0]) % NX * NZ + z, (y + d[1]) % NY * NC + (k + d[2]) % NC)

    barrier = pltpu.get_barrier_semaphore()
    peers = [z_peer(d) for d in Z_OFFS] + [xc_peer(d) for d in XC_OFFS]
    for peer in peers:
        pl.semaphore_signal(barrier, inc=1, device_id=peer, device_id_type=MESH)

    def put(group, src, dst, peer):
        pltpu.make_async_remote_copy(src, dst, send.at[group], recv.at[group], device_id=peer, device_id_type=MESH).start()

    def whole(group, ref):
        return pltpu.make_async_remote_copy(
            ref, ref, send.at[group], recv.at[group], device_id=x_peer(1), device_id_type=MESH
        )

    first, second = owners[0], owners[1]
    is_first = (row == first).astype(F32)
    is_second = (row == second).astype(F32)
    other = (1.0 - is_first) * (1.0 - is_second)

    block = fac[0].astype(F32) * is_second
    for ig in range(4):
        for jb in range(4):
            fmask[ig * 4 + jb] = block[ig * 16:ig * 16 + 16, jb * 128:jb * 128 + 128]
    ig = z // 4
    dmine[...] = diag[0, pl.ds(pl.multiple_of(ig * 16, 16), 16), :].astype(F32)

    place = dev[...] * 8 + blk[...]
    rows = lax.broadcasted_iota(jnp.int32, (512, 256), 0)
    hot = jnp.concatenate([(rows == place).astype(F32).astype(BF16), (rows == place + 4).astype(F32).astype(BF16)], axis=1)
    upper = jnp.concatenate(split(child[:, 0, :]), axis=1)
    lower = jnp.concatenate(split(child[:, 1, :]), axis=1)
    total = dot(hot, jnp.concatenate([upper, lower], axis=0))
    summed[...] = (total[:, :128] + total[:, 128:]).reshape(64, 8, 128)

    chosen = lax.broadcasted_iota(jnp.int32, (8, 128), 0) == col
    for b in range(4):
        order[b] = right[:, b * 128:b * 128 + 128]
        for kk in range(2):
            lines = jnp.where(chosen, order[b, pl.ds(kk, 8, stride=2), :], 0.0)
            rown[kk * 4 + b:kk * 4 + b + 1, :] = jnp.sum(lines, axis=0, keepdims=True)
    pown[0] = summed[first] + rown[...] * is_first
    pown[1] = summed[second] + rown[...] * is_second

    pl.semaphore_wait(barrier, len(peers))

    for s, d in enumerate(Z_OFFS):
        put(0, pown.at[0], pz.at[0, s], z_peer(d))
    for s, d in enumerate(Z_OFFS):
        put(2, fmask.at[(z + d) % NZ], fz.at[s], z_peer(d))
    for s, d in enumerate(Z_OFFS):
        put(1, pown.at[1], pz.at[1, s], z_peer(d))
    for d in C_OFFS:
        put(3, dmine, dg.at[col], c_peer(d))
    dg[col] = dmine[...]
    for s, d in enumerate(X_OFFS):
        put(4, summed.at[pl.ds((x + d) % NX * NZ, NZ)], mx.at[s], x_peer(d))

    def panel_sum(p):
        whole(p, pz.at[p]).wait_recv()
        pmine[p] = pown[p] + jnp.sum(pz[p], axis=0)
        for d in XC_OFFS:
            put(5 + p, pmine.at[p], px.at[p, (4 - d[0]) % 4 * 8 + col], xc_peer(d))
        px[p, col] = pmine[p]

    panel_sum(0)
    whole(2, fz).wait_recv()
    fmine[...] = fmask[z] + jnp.sum(fz[...], axis=0)
    for d in XC_OFFS:
        put(7, fmine, fx.at[(4 - d[0]) % 4 * 8 + col], xc_peer(d))
    fx[col] = fmine[...]
    panel_sum(1)
    whole(4, mx).wait_recv()
    mmine[...] = summed[pl.ds(x * NZ, NZ)] + mx[0] + mx[1] + mx[2]
    for s, d in enumerate(Z_OFFS):
        put(8, mmine.at[(z + d) % NZ], mz.at[s], z_peer(d))

    def panel_state(p):
        whole(5 + p, px.at[p, pl.ds(0, 31)]).wait_recv()
        value = px[p, 0:8] + px[p, 8:16] + px[p, 16:24] + px[p, 24:32]
        xs[p] = value.reshape(64, 128)
        return jnp.concatenate(
            [jnp.concatenate([xs[p, pl.ds(kk * 4 + b, 8, stride=8), :] for kk in range(2)], axis=0) for b in range(4)],
            axis=1,
        )

    eye = (
        lax.broadcasted_iota(jnp.int32, (64, 512), 1) == lax.broadcasted_iota(jnp.int32, (64, 512), 0) + col * 64
    ).astype(F32)
    w_first = (eye * is_first - fac[0].astype(F32) * other).astype(BF16)
    w_second = (eye * is_second - fac[1].astype(F32) * (1.0 - is_second) * (1.0 - is_first)).astype(BF16)

    state = stacked(panel_state(0))
    whole(3, dg.at[pl.ds(0, 7)]).wait_recv()
    group = folded(dot_t(state, dg[...].reshape(128, 512).astype(BF16)))
    whole(7, fx.at[pl.ds(0, 31)]).wait_recv()
    piece = (fx[0:8] + fx[8:16] + fx[16:24] + fx[24:32]).reshape(128, 128).astype(BF16)
    tz[z] = folded(dot(stacked(group), piece))
    for d in Z_OFFS:
        put(9, tz.at[z], tz.at[z], z_peer(d))

    solved = folded(dot_t(state, diag[0]))
    partial = folded(dot(stacked(solved), w_first))
    whole(8, mz).wait_recv()
    assembled = (mmine[z] + jnp.sum(mz[...], axis=0)) * other
    mine = lax.broadcasted_iota(jnp.int32, (8, 128), 0) == col
    placed = jnp.concatenate(
        [
            jnp.concatenate(
                [jnp.where(mine, assembled[kk * 4 + b:kk * 4 + b + 1, :], 0.0) for kk in range(2)], axis=0
            )
            for b in range(4)
        ],
        axis=1,
    )
    partial = partial + placed
    state = panel_state(1)

    whole(9, tz.at[pl.ds(0, 15)]).wait_recv()
    update = jnp.concatenate([tz[b] + tz[4 + b] + tz[8 + b] + tz[12 + b] for b in range(4)], axis=1)
    solved = folded(dot_t(stacked(state - update), diag[1]))
    part[...] = partial + folded(dot(stacked(solved), w_second))
    for s, d in enumerate(C_OFFS):
        put(10, part, pr.at[s], c_peer(d))
    whole(10, pr).wait_recv()
    total = part[...] + jnp.sum(pr[...], axis=0)
    for b in range(4):
        for kk in range(2):
            order[b, pl.ds(kk, 8, stride=2), :] = total[kk * 8:kk * 8 + 8, b * 128:b * 128 + 128]
        lanes = slice(b * 128, b * 128 + 128)
        out[:, lanes] = order[b] + right[:, lanes] * other

    whole(0, pz.at[0]).wait_send()
    whole(1, pz.at[1]).wait_send()
    whole(2, fz).wait_send()
    whole(3, dg.at[pl.ds(0, 7)]).wait_send()
    whole(4, mx).wait_send()
    whole(5, px.at[0, pl.ds(0, 31)]).wait_send()
    whole(6, px.at[1, pl.ds(0, 31)]).wait_send()
    whole(7, fx.at[pl.ds(0, 31)]).wait_send()
    whole(8, mz).wait_send()
    whole(9, tz.at[pl.ds(0, 15)]).wait_send()
    whole(10, pr).wait_send()


def body(right_side, child_updates, child_device, child_block, owners, diag_inverse, panel_factor):
    vmem = pl.BlockSpec(memory_space=pltpu.VMEM)
    return pl.pallas_call(
        kernel,
        out_shape=jax.ShapeDtypeStruct((16, 512), F32),
        in_specs=[pl.BlockSpec(memory_space=pltpu.SMEM)] + [vmem] * 6,
        out_specs=vmem,
        scratch_shapes=[
            pltpu.VMEM((64, 8, 128), F32),
            pltpu.VMEM((16, 16, 128), F32),
            pltpu.VMEM((15, 16, 128), F32),
            pltpu.VMEM((16, 128), F32),
            pltpu.VMEM((32, 16, 128), F32),
            pltpu.VMEM((2, 8, 128), F32),
            pltpu.VMEM((2, 15, 8, 128), F32),
            pltpu.VMEM((2, 8, 128), F32),
            pltpu.VMEM((2, 32, 8, 128), F32),
            pltpu.VMEM((16, 512), F32),
            pltpu.VMEM((8, 16, 512), F32),
            pltpu.VMEM((3, 16, 8, 128), F32),
            pltpu.VMEM((16, 8, 128), F32),
            pltpu.VMEM((15, 8, 128), F32),
            pltpu.VMEM((16, 16, 128), F32),
            pltpu.VMEM((16, 512), F32),
            pltpu.VMEM((7, 16, 512), F32),
            pltpu.VMEM((2, 64, 128), F32),
            pltpu.VMEM((8, 128), F32),
            pltpu.VMEM((4, 16, 128), F32),
            pltpu.SemaphoreType.DMA((11,)),
            pltpu.SemaphoreType.DMA((11,)),
        ],
        compiler_params=pltpu.CompilerParams(
            collective_id=0, has_side_effects=True, vmem_limit_bytes=32 * 1024 * 1024
        ),
    )(
        owners, right_side, child_updates, child_device.reshape(1, 256), child_block.reshape(1, 256),
        diag_inverse, panel_factor,
    )


def solution(mesh):
    return jax.shard_map(
        body,
        mesh=mesh,
        in_specs=(
            P(None, "rows"),
            P("rows", "cols", None),
            P("rows", None),
            P("rows", None),
            P(),
            P(None, "cols", None),
            P(None, "cols", "rows"),
        ),
        out_specs=P(None, "rows"),
        check_vma=False,
    )
```

time: 718 us -> 55.3 us (0.08)
  blocking collectives: 638 us -> 0 us
  Pallas kernels: 0 us -> 50.2 us
  starting transfers between devices: 29.2 us -> 0 us
  waiting for transfers between devices: 28.3 us -> 0 us
  local copies, waits for them, and re-layouts: 15.3 us -> 4.82 us
    psum x4 -> x0, blocking collectives: 484 us -> none  [the longest x2 441 us: broadcast(): return lax.psum(jnp.where(mine, shard, jnp.zeros_like(shard)), axis)]
    all_gather x3 -> x0, blocking collectives: 155 us -> none  [the longest x2 138 us: body(): solved = lax.all_gather(part_solution, 'cols', axis=1, tiled=True)]
    pallas_call x0 -> x1, Pallas kernels: none -> 50.2 us  [body(): pl.pallas_call(kernel, out_shape=jax.ShapeDtypeStruct((16, 512), F32), in...]
    all_to_all x2 -> x0, starting transfers between devices: 29.2 us -> none  [the longest x1 19.1 us: body(): lax.all_to_all(send_tags, 'rows', split_axis=0, concat_axis=0, tiled=True)]
    all_to_all x2 -> x0, waiting for transfers between devices: 28.3 us -> none  [the longest x1 23.8 us: body(): lax.all_to_all(send_vals, 'rows', split_axis=0, concat_axis=0, tiled=True)]
    scatter x2 -> x0, local copies, waits for them, and re-layouts: 8.36 us -> none  [the longest x1 6.96 us: body(): jnp.zeros((nrows * capacity, kc, blk), jnp.float32).at[places]]
  transfers between devices with their start and end apart: 2 -> 0, of which waited for: 2 -> 0; matrix products, arithmetic and copies ran while one was open for 1% -> 0% of each run, Pallas kernels for 0% -> 0%
where the time goes in v1:
time: 55.3 us; the launch traced here: 55 us
  Pallas kernels  50.2 us (91%)
  local copies, waits for them, and re-layouts  4.82 us (9%)
    pallas_call x1, Pallas kernels, body(): pl.pallas_call(kernel, out_shape=jax.ShapeDtypeStruct((16, 512), F32), in...  50.2 us
    unnamed x15, local copies, waits for them, and re-layouts  4.82 us

profile of v1, /device:TPU:1, one launch (start us, length us, event | category | flops | bytes accessed | tf_op | source)
XLA Modules:
  0.0 55.0 jit_solution(9727104564436668310)
XLA Ops:
  0.0 0.0 copy-start.5
  0.0 0.0 copy-start.4
  0.0 0.0 copy-start.6
  0.0 0.7 %copy-done.5 = s32[256,1]{0,1:T(1,128)S(1)} copy-done((s32[256,1]{0,1:T(1,128)S(1)}, s32[256,1]{0,1:T(1,128)}, u32[]{:S(2)}) %copy-start.5) | copy-done | bytes 1048
  0.7 0.0 copy-done.4
  0.7 0.0 copy-done.6
  0.7 0.0 copy-start
  0.7 0.9 %copy-done = f32[256,2,128]{2,1,0:T(2,128)S(1)} copy-done((f32[256,2,128]{2,1,0:T(2,128)S(1)}, f32[256,2,128]{2,1,0:T(2,128)}, u32[]{:S(2)}) %copy-start) | copy-done | bytes 262168
  1.6 0.0 copy-start.1
  1.7 0.9 %copy-done.1 = bf16[2,64,512]{2,1,0:T(8,128)(2,1)S(1)} copy-done((bf16[2,64,512]{2,1,0:T(8,128)(2,1)S(1)}, bf16[2,64,512]{2,1,0:T(8,128)(2,1)}, u32[]{:S(2)}) %copy-start.1) | copy-done | bytes 131096
  2.6 0.0 copy-start.2
  2.6 0.9 %copy-done.2 = bf16[2,64,512]{2,1,0:T(8,128)(2,1)S(1)} copy-done((bf16[2,64,512]{2,1,0:T(8,128)(2,1)S(1)}, bf16[2,64,512]{2,1,0:T(8,128)(2,1)}, u32[]{:S(2)}) %copy-start.2) | copy-done | bytes 131096
  3.5 0.0 copy-start.3
  3.5 0.8 %copy-done.3 = f32[16,512]{1,0:T(8,128)S(1)} copy-done((f32[16,512]{1,0:T(8,128)S(1)}, f32[16,512]{1,0:T(8,128)}, u32[]{:S(2)}) %copy-start.3) | copy-done | bytes 32792
  4.2 50.2 %shard_map.73 = f32[16,512]{1,0:T(8,128)S(1)} custom-call(s32[2]{0:T(128)S(1)} %copy-done.6, f32[16,512]{1,0:T(8,128)S(1)} %copy-done.3, f32[256,2,128]{2,1,0:T(2,128)S(1)} %copy-done, s32[1,256]{1,0:T(1,128)S(1)} %bitcast.2, s32[1,256]{1,0:T(1,128)S(1)} %bitcast.3, bf16[2,64,512]{2,1,0:T(8,128)(2,1)S(1)} %copy-done.1, bf16[2,64,512]{2,1,0:T(8,128)(2,1)S(1)} %copy-done.2), custom_call_target="tpu_custom_call" | custom-call | tf_op jit(solution)/shard_map/pallas_call | solution.py:206
  54.4 0.6 %copy.9 = f32[16,512]{1,0:T(8,128)} copy(f32[16,512]{1,0:T(8,128)S(1)} %shard_map.73) | data formatting | bytes 65536
Async XLA Ops:
  0.0 0.7 %copy-start.5 = (s32[256,1]{0,1:T(1,128)S(1)}, s32[256,1]{0,1:T(1,128)}, u32[]{:S(2)}) copy-start(s32[256,1]{0,1:T(1,128)} %param.10) | copy-start | bytes 3076
  0.0 0.7 %copy-start.4 = (s32[256,1]{0,1:T(1,128)S(1)}, s32[256,1]{0,1:T(1,128)}, u32[]{:S(2)}) copy-start(s32[256,1]{0,1:T(1,128)} %param.9) | copy-start | bytes 3076
  0.0 0.7 %copy-start.6 = (s32[2]{0:T(128)S(1)}, s32[2]{0:T(128)}, u32[]{:S(2)}) copy-start(s32[2]{0:T(128)} %owners.1) | copy-start | bytes 28
  0.7 1.0 %copy-start = (f32[256,2,128]{2,1,0:T(2,128)S(1)}, f32[256,2,128]{2,1,0:T(2,128)}, u32[]{:S(2)}) copy-start(f32[256,2,128]{2,1,0:T(2,128)} %child.1) | copy-start | bytes 786436
  1.6 0.9 %copy-start.1 = (bf16[2,64,512]{2,1,0:T(8,128)(2,1)S(1)}, bf16[2,64,512]{2,1,0:T(8,128)(2,1)}, u32[]{:S(2)}) copy-start(bf16[2,64,512]{2,1,0:T(8,128)(2,1)} %diag.1) | copy-start | bytes 393220
  2.6 0.9 %copy-start.2 = (bf16[2,64,512]{2,1,0:T(8,128)(2,1)S(1)}, bf16[2,64,512]{2,1,0:T(8,128)(2,1)}, u32[]{:S(2)}) copy-start(bf16[2,64,512]{2,1,0:T(8,128)(2,1)} %fac.1) | copy-start | bytes 393220
  3.5 0.8 %copy-start.3 = (f32[16,512]{1,0:T(8,128)S(1)}, f32[16,512]{1,0:T(8,128)}, u32[]{:S(2)}) copy-start(f32[16,512]{1,0:T(8,128)} %right.1) | copy-start | bytes 98308

commit v2 on v1

--- a/solution.py
+++ b/solution.py
@@ -11,6 +11,7 @@
 F32, BF16 = jnp.float32, jnp.bfloat16
 NX, NY, NC, NZ = 4, 4, 2, 16
 
+NEAR = (4, -4, 3, -3, 2, -2, 1, -1)
 Z_OFFS = (8, 7, 9, 6, 10, 5, 11, 4, 12, 3, 13, 2, 14, 1, 15)
 X_OFFS = (2, 1, 3)
 C_OFFS = tuple((dy, dk) for dy in (2, 1, 3, 0) for dk in (0, 1) if dy or dk)
@@ -40,14 +41,15 @@
 
 
 def kernel(
-    owners, right, child, dev, blk, diag, fac, out,
-    summed, fmask, fz, fmine, fx, pown, pz, pmine, px, dmine, dg, mx, mmine, mz, tz, part, pr, xs, rown, order, send, recv,
+    owners_any, right_any, child_any, dev_any, blk_any, diag_any, fac_any, out,
+    owners, right, child, dev, blk, diag, fac, local,
+    summed, fmask, fz, fmine, fx, pown, pz, pmine, px, dmine, dg, mx, mmine, mz, tz, part, pr, xs, rown, order, dfull, ffull, dhalf, fhalf, pside, pfar, frelay, fpass, send, recv,
 ):
     row, col = lax.axis_index("rows"), lax.axis_index("cols")
     x, z, y, k = row // NZ, row % NZ, col // NC, col % NC
 
     def z_peer(d):
-        return (x * NZ + (z + d) % NZ, col)
+        return (x * NZ + (z + d + NZ) % NZ, col)
 
     def x_peer(d):
         return ((x + d) % NX * NZ + z, col)
@@ -58,8 +60,20 @@
     def xc_peer(d):
         return ((x + d[0]) % NX * NZ + z, (y + d[1]) % NY * NC + (k + d[2]) % NC)
 
+    loads = [
+        pltpu.make_async_copy(src, dst, local.at[i])
+        for i, (src, dst) in enumerate(
+            [
+                (owners_any, owners), (fac_any.at[0], fac.at[0]), (dev_any, dev), (blk_any, blk), (child_any, child),
+                (right_any, right), (diag_any, diag), (fac_any.at[1], fac.at[1]),
+            ]
+        )
+    ]
+    for load in loads:
+        load.start()
+
     barrier = pltpu.get_barrier_semaphore()
-    peers = [z_peer(d) for d in Z_OFFS] + [xc_peer(d) for d in XC_OFFS]
+    peers = [z_peer(d) for d in NEAR] + [xc_peer(d) for d in XC_OFFS]
     for peer in peers:
         pl.semaphore_signal(barrier, inc=1, device_id=peer, device_id_type=MESH)
 
@@ -71,26 +85,29 @@
             ref, ref, send.at[group], recv.at[group], device_id=x_peer(1), device_id_type=MESH
         )
 
+    loads[0].wait()
     first, second = owners[0], owners[1]
     is_first = (row == first).astype(F32)
     is_second = (row == second).astype(F32)
     other = (1.0 - is_first) * (1.0 - is_second)
 
+    loads[1].wait()
     block = fac[0].astype(F32) * is_second
     for ig in range(4):
         for jb in range(4):
-            fmask[ig * 4 + jb] = block[ig * 16:ig * 16 + 16, jb * 128:jb * 128 + 128]
-    ig = z // 4
-    dmine[...] = diag[0, pl.ds(pl.multiple_of(ig * 16, 16), 16), :].astype(F32)
-
+            fmask[(ig * 4 + jb - z + NZ) % NZ] = block[ig * 16:ig * 16 + 16, jb * 128:jb * 128 + 128]
+    loads[2].wait()
+    loads[3].wait()
     place = dev[...] * 8 + blk[...]
     rows = lax.broadcasted_iota(jnp.int32, (512, 256), 0)
     hot = jnp.concatenate([(rows == place).astype(F32).astype(BF16), (rows == place + 4).astype(F32).astype(BF16)], axis=1)
+    loads[4].wait()
     upper = jnp.concatenate(split(child[:, 0, :]), axis=1)
     lower = jnp.concatenate(split(child[:, 1, :]), axis=1)
     total = dot(hot, jnp.concatenate([upper, lower], axis=0))
     summed[...] = (total[:, :128] + total[:, 128:]).reshape(64, 8, 128)
 
+    loads[5].wait()
     chosen = lax.broadcasted_iota(jnp.int32, (8, 128), 0) == col
     for b in range(4):
         order[b] = right[:, b * 128:b * 128 + 128]
@@ -100,30 +117,60 @@
     pown[0] = summed[first] + rown[...] * is_first
     pown[1] = summed[second] + rown[...] * is_second
 
+    loads[6].wait()
+    ig = z // 4
+    dmine[...] = diag[0, pl.ds(pl.multiple_of(ig * 16, 16), 16), :].astype(F32)
+    dfull[col] = diag[1].astype(F32)
+    loads[7].wait()
+    ffull[col] = fac[1].astype(F32)
+
     pl.semaphore_wait(barrier, len(peers))
 
-    for s, d in enumerate(Z_OFFS):
+    for s, d in enumerate(NEAR):
         put(0, pown.at[0], pz.at[0, s], z_peer(d))
-    for s, d in enumerate(Z_OFFS):
-        put(2, fmask.at[(z + d) % NZ], fz.at[s], z_peer(d))
-    for s, d in enumerate(Z_OFFS):
+    put(2, fmask.at[pl.ds(5, 4)], frelay.at[pl.ds(0, 4)], z_peer(4))
+    put(2, fmask.at[pl.ds(9, 3)], frelay.at[pl.ds(4, 3)], z_peer(-4))
+    for s, d in enumerate(NEAR):
         put(1, pown.at[1], pz.at[1, s], z_peer(d))
     for d in C_OFFS:
         put(3, dmine, dg.at[col], c_peer(d))
     dg[col] = dmine[...]
     for s, d in enumerate(X_OFFS):
         put(4, summed.at[pl.ds((x + d) % NX * NZ, NZ)], mx.at[s], x_peer(d))
+    for group, full in ((11, dfull), (12, ffull)):
+        for d in (2, 1, 3):
+            put(group, full.at[col], full.at[col], c_peer((d, 0)))
+
+    def panel_near(p):
+        whole(p, pz.at[p]).wait_recv()
+        above = pz[p, 1] + pz[p, 3] + pz[p, 5] + pz[p, 7]
+        below = pz[p, 2] + pz[p, 4] + pz[p, 6]
+        pside[p, 0] = below
+        pside[p, 1] = above
+        put(15 + p, pside.at[p, 0], pfar.at[p, 0], z_peer(4))
+        put(15 + p, pside.at[p, 1], pfar.at[p, 1], z_peer(-4))
+        pmine[p] = pown[p] + above + below + pz[p, 0]
 
     def panel_sum(p):
-        whole(p, pz.at[p]).wait_recv()
-        pmine[p] = pown[p] + jnp.sum(pz[p], axis=0)
+        whole(15 + p, pfar.at[p]).wait_recv()
+        pmine[p] = pmine[p] + pfar[p, 0] + pfar[p, 1]
         for d in XC_OFFS:
             put(5 + p, pmine.at[p], px.at[p, (4 - d[0]) % 4 * 8 + col], xc_peer(d))
         px[p, col] = pmine[p]
 
+    panel_near(0)
+    whole(2, frelay).wait_recv()
+    for s, d in enumerate(NEAR):
+        if d == -4:
+            fpass[s] = fmask[12]
+        else:
+            fpass[s] = fmask[d % NZ] + frelay[d - 1 if d > 0 else 7 + d]
+        put(17, fpass.at[s], fz.at[s], z_peer(d))
+    panel_near(1)
+
     panel_sum(0)
-    whole(2, fz).wait_recv()
-    fmine[...] = fmask[z] + jnp.sum(fz[...], axis=0)
+    whole(17, fz).wait_recv()
+    fmine[...] = fmask[0] + jnp.sum(fz[...], axis=0)
     for d in XC_OFFS:
         put(7, fmine, fx.at[(4 - d[0]) % 4 * 8 + col], xc_peer(d))
     fx[col] = fmine[...]
@@ -146,7 +193,6 @@
         lax.broadcasted_iota(jnp.int32, (64, 512), 1) == lax.broadcasted_iota(jnp.int32, (64, 512), 0) + col * 64
     ).astype(F32)
     w_first = (eye * is_first - fac[0].astype(F32) * other).astype(BF16)
-    w_second = (eye * is_second - fac[1].astype(F32) * (1.0 - is_second) * (1.0 - is_first)).astype(BF16)
 
     state = stacked(panel_state(0))
     whole(3, dg.at[pl.ds(0, 7)]).wait_recv()
@@ -171,17 +217,26 @@
         ],
         axis=1,
     )
-    partial = partial + placed
+    part[...] = partial + placed
+    for s, d in enumerate(C_OFFS):
+        put(10, part, pr.at[s], c_peer(d))
+    for group, full in ((11, dfull), (12, ffull)):
+        whole(group, full.at[pl.ds(0, 3)]).wait_recv()
+        for d in range(4):
+            index = (y + d) % NY * NC + k
+            put(group + 2, full.at[index], full.at[index], c_peer((0, 1)))
     state = panel_state(1)
+    whole(13, dfull.at[pl.ds(0, 4)]).wait_recv()
+    dhalf[...] = dfull[...].reshape(512, 512).astype(BF16)
+    whole(14, ffull.at[pl.ds(0, 4)]).wait_recv()
+    fhalf[...] = ffull[...].reshape(512, 512).astype(BF16)
+    whole(10, pr).wait_recv()
+    total = part[...] + jnp.sum(pr[...], axis=0)
 
     whole(9, tz.at[pl.ds(0, 15)]).wait_recv()
     update = jnp.concatenate([tz[b] + tz[4 + b] + tz[8 + b] + tz[12 + b] for b in range(4)], axis=1)
-    solved = folded(dot_t(stacked(state - update), diag[1]))
-    part[...] = partial + folded(dot(stacked(solved), w_second))
-    for s, d in enumerate(C_OFFS):
-        put(10, part, pr.at[s], c_peer(d))
-    whole(10, pr).wait_recv()
-    total = part[...] + jnp.sum(pr[...], axis=0)
+    solved = folded(dot_t(stacked(state - update), dhalf[...]))
+    total = total + solved * is_second - folded(dot(stacked(solved), fhalf[...])) * other
     for b in range(4):
         for kk in range(2):
             order[b, pl.ds(kk, 8, stride=2), :] = total[kk * 8:kk * 8 + 8, b * 128:b * 128 + 128]
@@ -190,7 +245,10 @@
 
     whole(0, pz.at[0]).wait_send()
     whole(1, pz.at[1]).wait_send()
-    whole(2, fz).wait_send()
+    whole(2, frelay).wait_send()
+    whole(15, pfar.at[0]).wait_send()
+    whole(16, pfar.at[1]).wait_send()
+    whole(17, fz).wait_send()
     whole(3, dg.at[pl.ds(0, 7)]).wait_send()
     whole(4, mx).wait_send()
     whole(5, px.at[0, pl.ds(0, 31)]).wait_send()
@@ -199,23 +257,33 @@
     whole(8, mz).wait_send()
     whole(9, tz.at[pl.ds(0, 15)]).wait_send()
     whole(10, pr).wait_send()
+    for group, full in ((11, dfull), (12, ffull)):
+        whole(group, full.at[pl.ds(0, 3)]).wait_send()
+        whole(group + 2, full.at[pl.ds(0, 4)]).wait_send()
 
 
 def body(right_side, child_updates, child_device, child_block, owners, diag_inverse, panel_factor):
-    vmem = pl.BlockSpec(memory_space=pltpu.VMEM)
     return pl.pallas_call(
         kernel,
         out_shape=jax.ShapeDtypeStruct((16, 512), F32),
-        in_specs=[pl.BlockSpec(memory_space=pltpu.SMEM)] + [vmem] * 6,
-        out_specs=vmem,
+        in_specs=[pl.BlockSpec(memory_space=pltpu.HBM)] * 7,
+        out_specs=pl.BlockSpec(memory_space=pltpu.VMEM),
         scratch_shapes=[
+            pltpu.SMEM((2,), jnp.int32),
+            pltpu.VMEM((16, 512), F32),
+            pltpu.VMEM((256, 2, 128), F32),
+            pltpu.VMEM((1, 256), jnp.int32),
+            pltpu.VMEM((1, 256), jnp.int32),
+            pltpu.VMEM((2, 64, 512), BF16),
+            pltpu.VMEM((2, 64, 512), BF16),
+            pltpu.SemaphoreType.DMA((8,)),
             pltpu.VMEM((64, 8, 128), F32),
             pltpu.VMEM((16, 16, 128), F32),
-            pltpu.VMEM((15, 16, 128), F32),
+            pltpu.VMEM((8, 16, 128), F32),
             pltpu.VMEM((16, 128), F32),
             pltpu.VMEM((32, 16, 128), F32),
             pltpu.VMEM((2, 8, 128), F32),
-            pltpu.VMEM((2, 15, 8, 128), F32),
+            pltpu.VMEM((2, 8, 8, 128), F32),
             pltpu.VMEM((2, 8, 128), F32),
             pltpu.VMEM((2, 32, 8, 128), F32),
             pltpu.VMEM((16, 512), F32),
@@ -229,11 +297,19 @@
             pltpu.VMEM((2, 64, 128), F32),
             pltpu.VMEM((8, 128), F32),
             pltpu.VMEM((4, 16, 128), F32),
-            pltpu.SemaphoreType.DMA((11,)),
-            pltpu.SemaphoreType.DMA((11,)),
+            pltpu.VMEM((8, 64, 512), F32),
+            pltpu.VMEM((8, 64, 512), F32),
+            pltpu.VMEM((512, 512), BF16),
+            pltpu.VMEM((512, 512), BF16),
+            pltpu.VMEM((2, 2, 8, 128), F32),
+            pltpu.VMEM((2, 2, 8, 128), F32),
+            pltpu.VMEM((7, 16, 128), F32),
+            pltpu.VMEM((8, 16, 128), F32),
+            pltpu.SemaphoreType.DMA((18,)),
+            pltpu.SemaphoreType.DMA((18,)),
         ],
         compiler_params=pltpu.CompilerParams(
-            collective_id=0, has_side_effects=True, vmem_limit_bytes=32 * 1024 * 1024
+            collective_id=0, has_side_effects=True, vmem_limit_bytes=60 * 1024 * 1024
         ),
     )(
         owners, right_side, child_updates, child_device.reshape(1, 256), child_block.reshape(1, 256),

time: 55.3 us -> 48.7 us (0.88)
  local copies, waits for them, and re-layouts: 4.82 us -> 1.38 us
  Pallas kernels: 50.2 us -> 47.1 us
    unnamed x15 -> x1, local copies, waits for them, and re-layouts: 4.82 us -> 1.38 us
    pallas_call x1, Pallas kernels: 50.2 us -> 47.1 us  [body(): pl.pallas_call(kernel, out_shape=jax.ShapeDtypeStruct((16, 512), F32), in...]
where the time goes in v2:
time: 48.7 us; the launch traced here: 48.5 us
  Pallas kernels  47.1 us (97%)
  local copies, waits for them, and re-layouts  1.38 us (3%)
    pallas_call x1, Pallas kernels, body(): pl.pallas_call(kernel, out_shape=jax.ShapeDtypeStruct((16, 512), F32), in...  47.1 us
    unnamed x1, local copies, waits for them, and re-layouts  1.38 us

profile of v2, /device:TPU:1, one launch (start us, length us, event | category | flops | bytes accessed | tf_op | source)
XLA Modules:
  0.0 48.5 jit_solution(15580558752483770059)
XLA Ops:
  0.0 47.1 %shard_map.73 = f32[16,512]{1,0:T(8,128)} custom-call(s32[2]{0:T(128)} %owners_any.1, f32[16,512]{1,0:T(8,128)} %right_any.1, f32[256,2,128]{2,1,0:T(2,128)} %child_any.1, s32[1,256]{1,0:T(1,128)} %bitcast.2, s32[1,256]{1,0:T(1,128)} %bitcast.3, bf16[2,64,512]{2,1,0:T(8,128)(2,1)} %diag_any.1, bf16[2,64,512]{2,1,0:T(8,128)(2,1)} %fac_any.1), custom_call_target="tpu_custom_call" | custom-call | tf_op jit(solution)/shard_map/pallas_call | solution.py:266
  47.1 1.4 %copy.9 = f32[16,512]{1,0:T(8,128)} copy(f32[16,512]{1,0:T(8,128)} %shard_map.73) | data formatting | bytes 65536

commit v3 on v2

--- a/solution.py
+++ b/solution.py
@@ -11,7 +11,10 @@
 F32, BF16 = jnp.float32, jnp.bfloat16
 NX, NY, NC, NZ = 4, 4, 2, 16
 
+EARLY, MIDDLE, LATE = (0, 1, 2), (3,), ()
+
 NEAR = (4, -4, 3, -3, 2, -2, 1, -1)
+RELAY = (4, -3, 3, -2, 2, -1, 1)
 Z_OFFS = (8, 7, 9, 6, 10, 5, 11, 4, 12, 3, 13, 2, 14, 1, 15)
 X_OFFS = (2, 1, 3)
 C_OFFS = tuple((dy, dk) for dy in (2, 1, 3, 0) for dk in (0, 1) if dy or dk)
@@ -43,7 +46,7 @@
 def kernel(
     owners_any, right_any, child_any, dev_any, blk_any, diag_any, fac_any, out,
     owners, right, child, dev, blk, diag, fac, local,
-    summed, fmask, fz, fmine, fx, pown, pz, pmine, px, dmine, dg, mx, mmine, mz, tz, part, pr, xs, rown, order, dfull, ffull, dhalf, fhalf, pside, pfar, frelay, fpass, send, recv,
+    summed, fmask, fz, fmine, fx, pown, pz, pmine, px, dg, mx, mmine, mz, tz, part, pr, xs, rown, order, dfull, ffull, dhalf, fhalf, pside, pfar, frelay, fpass, send, recv,
 ):
     row, col = lax.axis_index("rows"), lax.axis_index("cols")
     x, z, y, k = row // NZ, row % NZ, col // NC, col % NC
@@ -79,6 +82,9 @@
 
     def put(group, src, dst, peer):
         pltpu.make_async_remote_copy(src, dst, send.at[group], recv.at[group], device_id=peer, device_id_type=MESH).start()
+
+    def relay_group(e):
+        return 19 + RELAY.index(e)
 
     def whole(group, ref):
         return pltpu.make_async_remote_copy(
@@ -119,7 +125,7 @@
 
     loads[6].wait()
     ig = z // 4
-    dmine[...] = diag[0, pl.ds(pl.multiple_of(ig * 16, 16), 16), :].astype(F32)
+    dg[col] = diag[0, pl.ds(pl.multiple_of(ig * 16, 16), 16), :].astype(F32)
     dfull[col] = diag[1].astype(F32)
     loads[7].wait()
     ffull[col] = fac[1].astype(F32)
@@ -128,18 +134,36 @@
 
     for s, d in enumerate(NEAR):
         put(0, pown.at[0], pz.at[0, s], z_peer(d))
-    put(2, fmask.at[pl.ds(5, 4)], frelay.at[pl.ds(0, 4)], z_peer(4))
-    put(2, fmask.at[pl.ds(9, 3)], frelay.at[pl.ds(4, 3)], z_peer(-4))
-    for s, d in enumerate(NEAR):
-        put(1, pown.at[1], pz.at[1, s], z_peer(d))
-    for d in C_OFFS:
-        put(3, dmine, dg.at[col], c_peer(d))
-    dg[col] = dmine[...]
+    for e in RELAY:
+        far = 4 if e > 0 else -4
+        put(relay_group(e), fmask.at[(e + far) % NZ], frelay.at[e % 8], z_peer(far))
+    put(17, fmask.at[12], fz.at[7], z_peer(-4))
+    for d in (2, 1, 3):
+        put(3, dg.at[col], dg.at[col], c_peer((d, 0)))
     for s, d in enumerate(X_OFFS):
         put(4, summed.at[pl.ds((x + d) % NX * NZ, NZ)], mx.at[s], x_peer(d))
-    for group, full in ((11, dfull), (12, ffull)):
-        for d in (2, 1, 3):
-            put(group, full.at[col], full.at[col], c_peer((d, 0)))
+    def half(part, index):
+        return (dfull if part < 2 else ffull).at[index, pl.ds(part % 2 * 32, 32)]
+
+    def halves(part):
+        return (dfull if part < 2 else ffull).at[pl.ds(0, 4), pl.ds(0, 32)]
+
+    def three(part):
+        return (dfull if part < 2 else ffull).at[pl.ds(0, 3), pl.ds(0, 32)]
+
+    def gather(parts):
+        for part in parts:
+            for d in (2, 1, 3):
+                put(26 + part, half(part, col), half(part, col), c_peer((d, 0)))
+
+    def forward(parts):
+        for part in parts:
+            whole(26 + part, three(part)).wait_recv()
+            for d in range(4):
+                index = (y + d) % NY * NC + k
+                put(30 + part, half(part, index), half(part, index), c_peer((0, 1)))
+
+    gather(EARLY)
 
     def panel_near(p):
         whole(p, pz.at[p]).wait_recv()
@@ -159,22 +183,24 @@
         px[p, col] = pmine[p]
 
     panel_near(0)
-    whole(2, frelay).wait_recv()
+    for s, e in enumerate(RELAY):
+        whole(relay_group(e), frelay.at[e % 8]).wait_recv()
+        fpass[s] = fmask[e % NZ] + frelay[e % 8]
+        put(17, fpass.at[s], fz.at[s], z_peer(e))
     for s, d in enumerate(NEAR):
-        if d == -4:
-            fpass[s] = fmask[12]
-        else:
-            fpass[s] = fmask[d % NZ] + frelay[d - 1 if d > 0 else 7 + d]
-        put(17, fpass.at[s], fz.at[s], z_peer(d))
-    panel_near(1)
-
+        put(1, pown.at[1], pz.at[1, s], z_peer(d))
+
+    whole(3, dg.at[pl.ds(0, 3)]).wait_recv()
+    for d in range(4):
+        index = (y + d) % NY * NC + k
+        put(18, dg.at[index], dg.at[index], c_peer((0, 1)))
     panel_sum(0)
     whole(17, fz).wait_recv()
     fmine[...] = fmask[0] + jnp.sum(fz[...], axis=0)
     for d in XC_OFFS:
         put(7, fmine, fx.at[(4 - d[0]) % 4 * 8 + col], xc_peer(d))
     fx[col] = fmine[...]
-    panel_sum(1)
+    panel_near(1)
     whole(4, mx).wait_recv()
     mmine[...] = summed[pl.ds(x * NZ, NZ)] + mx[0] + mx[1] + mx[2]
     for s, d in enumerate(Z_OFFS):
@@ -195,13 +221,16 @@
     w_first = (eye * is_first - fac[0].astype(F32) * other).astype(BF16)
 
     state = stacked(panel_state(0))
-    whole(3, dg.at[pl.ds(0, 7)]).wait_recv()
+    whole(18, dg.at[pl.ds(0, 4)]).wait_recv()
     group = folded(dot_t(state, dg[...].reshape(128, 512).astype(BF16)))
+    panel_sum(1)
+    gather(MIDDLE)
     whole(7, fx.at[pl.ds(0, 31)]).wait_recv()
     piece = (fx[0:8] + fx[8:16] + fx[16:24] + fx[24:32]).reshape(128, 128).astype(BF16)
     tz[z] = folded(dot(stacked(group), piece))
     for d in Z_OFFS:
         put(9, tz.at[z], tz.at[z], z_peer(d))
+    gather(LATE)
 
     solved = folded(dot_t(state, diag[0]))
     partial = folded(dot(stacked(solved), w_first))
@@ -220,18 +249,16 @@
     part[...] = partial + placed
     for s, d in enumerate(C_OFFS):
         put(10, part, pr.at[s], c_peer(d))
-    for group, full in ((11, dfull), (12, ffull)):
-        whole(group, full.at[pl.ds(0, 3)]).wait_recv()
-        for d in range(4):
-            index = (y + d) % NY * NC + k
-            put(group + 2, full.at[index], full.at[index], c_peer((0, 1)))
+    forward(EARLY)
     state = panel_state(1)
-    whole(13, dfull.at[pl.ds(0, 4)]).wait_recv()
-    dhalf[...] = dfull[...].reshape(512, 512).astype(BF16)
-    whole(14, ffull.at[pl.ds(0, 4)]).wait_recv()
-    fhalf[...] = ffull[...].reshape(512, 512).astype(BF16)
+    forward(MIDDLE)
     whole(10, pr).wait_recv()
     total = part[...] + jnp.sum(pr[...], axis=0)
+    forward(LATE)
+    for part_ in range(4):
+        whole(30 + part_, halves(part_)).wait_recv()
+    dhalf[...] = dfull[...].reshape(512, 512).astype(BF16)
+    fhalf[...] = ffull[...].reshape(512, 512).astype(BF16)
 
     whole(9, tz.at[pl.ds(0, 15)]).wait_recv()
     update = jnp.concatenate([tz[b] + tz[4 + b] + tz[8 + b] + tz[12 + b] for b in range(4)], axis=1)
@@ -245,11 +272,13 @@
 
     whole(0, pz.at[0]).wait_send()
     whole(1, pz.at[1]).wait_send()
-    whole(2, frelay).wait_send()
+    for e in RELAY:
+        whole(relay_group(e), frelay.at[e % 8]).wait_send()
     whole(15, pfar.at[0]).wait_send()
     whole(16, pfar.at[1]).wait_send()
     whole(17, fz).wait_send()
-    whole(3, dg.at[pl.ds(0, 7)]).wait_send()
+    whole(3, dg.at[pl.ds(0, 3)]).wait_send()
+    whole(18, dg.at[pl.ds(0, 4)]).wait_send()
     whole(4, mx).wait_send()
     whole(5, px.at[0, pl.ds(0, 31)]).wait_send()
     whole(6, px.at[1, pl.ds(0, 31)]).wait_send()
@@ -257,9 +286,9 @@
     whole(8, mz).wait_send()
     whole(9, tz.at[pl.ds(0, 15)]).wait_send()
     whole(10, pr).wait_send()
-    for group, full in ((11, dfull), (12, ffull)):
-        whole(group, full.at[pl.ds(0, 3)]).wait_send()
-        whole(group + 2, full.at[pl.ds(0, 4)]).wait_send()
+    for part_ in range(4):
+        whole(26 + part_, three(part_)).wait_send()
+        whole(30 + part_, halves(part_)).wait_send()
 
 
 def body(right_side, child_updates, child_device, child_block, owners, diag_inverse, panel_factor):
@@ -286,7 +315,6 @@
             pltpu.VMEM((2, 8, 8, 128), F32),
             pltpu.VMEM((2, 8, 128), F32),
             pltpu.VMEM((2, 32, 8, 128), F32),
-            pltpu.VMEM((16, 512), F32),
             pltpu.VMEM((8, 16, 512), F32),
             pltpu.VMEM((3, 16, 8, 128), F32),
             pltpu.VMEM((16, 8, 128), F32),
@@ -303,10 +331,10 @@
             pltpu.VMEM((512, 512), BF16),
             pltpu.VMEM((2, 2, 8, 128), F32),
             pltpu.VMEM((2, 2, 8, 128), F32),
+            pltpu.VMEM((8, 16, 128), F32),
             pltpu.VMEM((7, 16, 128), F32),
-            pltpu.VMEM((8, 16, 128), F32),
-            pltpu.SemaphoreType.DMA((18,)),
-            pltpu.SemaphoreType.DMA((18,)),
+            pltpu.SemaphoreType.DMA((34,)),
+            pltpu.SemaphoreType.DMA((34,)),
         ],
         compiler_params=pltpu.CompilerParams(
             collective_id=0, has_side_effects=True, vmem_limit_bytes=60 * 1024 * 1024

time: 48.7 us -> 43.9 us (0.901)
  Pallas kernels: 47.1 us -> 42.3 us
    pallas_call x1, Pallas kernels: 47.1 us -> 42.3 us  [body(): pl.pallas_call(kernel, out_shape=jax.ShapeDtypeStruct((16, 512), F32), in...]
where the time goes in v3:
time: 43.9 us; the launch traced here: 43.7 us
  Pallas kernels  42.3 us (96%)
  local copies, waits for them, and re-layouts  1.38 us (3%)
    pallas_call x1, Pallas kernels, body(): pl.pallas_call(kernel, out_shape=jax.ShapeDtypeStruct((16, 512), F32), in...  42.3 us
    unnamed x1, local copies, waits for them, and re-layouts  1.38 us

profile of v3, /device:TPU:1, one launch (start us, length us, event | category | flops | bytes accessed | tf_op | source)
XLA Modules:
  0.0 43.7 jit_solution(2000100002568733193)
XLA Ops:
  0.0 42.3 %shard_map.73 = f32[16,512]{1,0:T(8,128)} custom-call(s32[2]{0:T(128)} %owners_any.1, f32[16,512]{1,0:T(8,128)} %right_any.1, f32[256,2,128]{2,1,0:T(2,128)} %child_any.1, s32[1,256]{1,0:T(1,128)} %bitcast.2, s32[1,256]{1,0:T(1,128)} %bitcast.3, bf16[2,64,512]{2,1,0:T(8,128)(2,1)} %diag_any.1, bf16[2,64,512]{2,1,0:T(8,128)(2,1)} %fac_any.1), custom_call_target="tpu_custom_call" | custom-call | tf_op jit(solution)/shard_map/pallas_call | solution.py:295
  42.3 1.4 %copy.9 = f32[16,512]{1,0:T(8,128)} copy(f32[16,512]{1,0:T(8,128)} %shard_map.73) | data formatting | bytes 65536

commit v4 on v3

--- a/solution.py
+++ b/solution.py
@@ -46,7 +46,7 @@
 def kernel(
     owners_any, right_any, child_any, dev_any, blk_any, diag_any, fac_any, out,
     owners, right, child, dev, blk, diag, fac, local,
-    summed, fmask, fz, fmine, fx, pown, pz, pmine, px, dg, mx, mmine, mz, tz, part, pr, xs, rown, order, dfull, ffull, dhalf, fhalf, pside, pfar, frelay, fpass, send, recv,
+    summed, fmask, fz, fmine, fx, pown, pz, pmine, px, dg, mx, mmine, mz, tz, part, pr, pair, xs, rown, order, dfull, ffull, dhalf, fhalf, pside, pfar, frelay, fpass, send, recv,
 ):
     row, col = lax.axis_index("rows"), lax.axis_index("cols")
     x, z, y, k = row // NZ, row % NZ, col // NC, col % NC
@@ -247,22 +247,26 @@
         axis=1,
     )
     part[...] = partial + placed
-    for s, d in enumerate(C_OFFS):
-        put(10, part, pr.at[s], c_peer(d))
+    put(10, part, pair, c_peer((0, 1)))
     forward(EARLY)
+    whole(10, pair).wait_recv()
+    whole(10, pair).wait_send()
+    part[...] = part[...] + pair[...]
+    for s, d in enumerate((2, 1, 3)):
+        put(11, part, pr.at[s], c_peer((d, 0)))
     state = panel_state(1)
     forward(MIDDLE)
-    whole(10, pr).wait_recv()
+    whole(11, pr).wait_recv()
     total = part[...] + jnp.sum(pr[...], axis=0)
     forward(LATE)
     for part_ in range(4):
         whole(30 + part_, halves(part_)).wait_recv()
-    dhalf[...] = dfull[...].reshape(512, 512).astype(BF16)
+    dhalf[...] = dfull[...].reshape(512, 512).T.astype(BF16)
     fhalf[...] = ffull[...].reshape(512, 512).astype(BF16)
 
     whole(9, tz.at[pl.ds(0, 15)]).wait_recv()
     update = jnp.concatenate([tz[b] + tz[4 + b] + tz[8 + b] + tz[12 + b] for b in range(4)], axis=1)
-    solved = folded(dot_t(stacked(state - update), dhalf[...]))
+    solved = folded(dot(stacked(state - update), dhalf[...]))
     total = total + solved * is_second - folded(dot(stacked(solved), fhalf[...])) * other
     for b in range(4):
         for kk in range(2):
@@ -285,7 +289,7 @@
     whole(7, fx.at[pl.ds(0, 31)]).wait_send()
     whole(8, mz).wait_send()
     whole(9, tz.at[pl.ds(0, 15)]).wait_send()
-    whole(10, pr).wait_send()
+    whole(11, pr).wait_send()
     for part_ in range(4):
         whole(26 + part_, three(part_)).wait_send()
         whole(30 + part_, halves(part_)).wait_send()
@@ -321,7 +325,8 @@
             pltpu.VMEM((15, 8, 128), F32),
             pltpu.VMEM((16, 16, 128), F32),
             pltpu.VMEM((16, 512), F32),
-            pltpu.VMEM((7, 16, 512), F32),
+            pltpu.VMEM((3, 16, 512), F32),
+            pltpu.VMEM((16, 512), F32),
             pltpu.VMEM((2, 64, 128), F32),
             pltpu.VMEM((8, 128), F32),
             pltpu.VMEM((4, 16, 128), F32),

time: 43.9 us -> 43.1 us (0.982)
  Pallas kernels: 42.3 us -> 41.2 us
    pallas_call x1, Pallas kernels: 42.3 us -> 41.2 us  [body(): pl.pallas_call(kernel, out_shape=jax.ShapeDtypeStruct((16, 512), F32), in...]
where the time goes in v4:
time: 43.1 us; the launch traced here: 42.5 us
  Pallas kernels  41.2 us (96%)
  local copies, waits for them, and re-layouts  1.38 us (3%)
    pallas_call x1, Pallas kernels, body(): pl.pallas_call(kernel, out_shape=jax.ShapeDtypeStruct((16, 512), F32), in...  41.2 us
    unnamed x1, local copies, waits for them, and re-layouts  1.38 us

profile of v4, /device:TPU:1, one launch (start us, length us, event | category | flops | bytes accessed | tf_op | source)
XLA Modules:
  0.0 42.5 jit_solution(7363872605581547911)
XLA Ops:
  0.0 41.2 %shard_map.73 = f32[16,512]{1,0:T(8,128)} custom-call(s32[2]{0:T(128)} %owners_any.1, f32[16,512]{1,0:T(8,128)} %right_any.1, f32[256,2,128]{2,1,0:T(2,128)} %child_any.1, s32[1,256]{1,0:T(1,128)} %bitcast.2, s32[1,256]{1,0:T(1,128)} %bitcast.3, bf16[2,64,512]{2,1,0:T(8,128)(2,1)} %diag_any.1, bf16[2,64,512]{2,1,0:T(8,128)(2,1)} %fac_any.1), custom_call_target="tpu_custom_call" | custom-call | tf_op jit(solution)/shard_map/pallas_call | solution.py:299
  41.2 1.4 %copy.9 = f32[16,512]{1,0:T(8,128)} copy(f32[16,512]{1,0:T(8,128)} %shard_map.73) | data formatting | bytes 65536

commit v5 on v4

--- a/solution.py
+++ b/solution.py
@@ -138,8 +138,6 @@
         far = 4 if e > 0 else -4
         put(relay_group(e), fmask.at[(e + far) % NZ], frelay.at[e % 8], z_peer(far))
     put(17, fmask.at[12], fz.at[7], z_peer(-4))
-    for d in (2, 1, 3):
-        put(3, dg.at[col], dg.at[col], c_peer((d, 0)))
     for s, d in enumerate(X_OFFS):
         put(4, summed.at[pl.ds((x + d) % NX * NZ, NZ)], mx.at[s], x_peer(d))
     def half(part, index):
@@ -163,7 +161,10 @@
                 index = (y + d) % NY * NC + k
                 put(30 + part, half(part, index), half(part, index), c_peer((0, 1)))
 
-    gather(EARLY)
+    gather(EARLY[:1])
+    for d in (2, 1, 3):
+        put(3, dg.at[col], dg.at[col], c_peer((d, 0)))
+    gather(EARLY[1:])
 
     def panel_near(p):
         whole(p, pz.at[p]).wait_recv()
@@ -190,16 +191,16 @@
     for s, d in enumerate(NEAR):
         put(1, pown.at[1], pz.at[1, s], z_peer(d))
 
-    whole(3, dg.at[pl.ds(0, 3)]).wait_recv()
-    for d in range(4):
-        index = (y + d) % NY * NC + k
-        put(18, dg.at[index], dg.at[index], c_peer((0, 1)))
     panel_sum(0)
     whole(17, fz).wait_recv()
     fmine[...] = fmask[0] + jnp.sum(fz[...], axis=0)
     for d in XC_OFFS:
         put(7, fmine, fx.at[(4 - d[0]) % 4 * 8 + col], xc_peer(d))
     fx[col] = fmine[...]
+    whole(3, dg.at[pl.ds(0, 3)]).wait_recv()
+    for d in range(4):
+        index = (y + d) % NY * NC + k
+        put(18, dg.at[index], dg.at[index], c_peer((0, 1)))
     panel_near(1)
     whole(4, mx).wait_recv()
     mmine[...] = summed[pl.ds(x * NZ, NZ)] + mx[0] + mx[1] + mx[2]

time: 43.1 us -> 43.1 us (level)
  no operation moved by 1% of the time
where the time goes in v5:
time: 43.1 us; the launch traced here: 42.5 us
  Pallas kernels  41.2 us (96%)
  local copies, waits for them, and re-layouts  1.38 us (3%)
    pallas_call x1, Pallas kernels, body(): pl.pallas_call(kernel, out_shape=jax.ShapeDtypeStruct((16, 512), F32), in...  41.2 us
    unnamed x1, local copies, waits for them, and re-layouts  1.38 us

profile of v5, /device:TPU:1, one launch (start us, length us, event | category | flops | bytes accessed | tf_op | source)
XLA Modules:
  0.0 42.5 jit_solution(15439059153903550196)
XLA Ops:
  0.0 41.2 %shard_map.73 = f32[16,512]{1,0:T(8,128)} custom-call(s32[2]{0:T(128)} %owners_any.1, f32[16,512]{1,0:T(8,128)} %right_any.1, f32[256,2,128]{2,1,0:T(2,128)} %child_any.1, s32[1,256]{1,0:T(1,128)} %bitcast.2, s32[1,256]{1,0:T(1,128)} %bitcast.3, bf16[2,64,512]{2,1,0:T(8,128)(2,1)} %diag_any.1, bf16[2,64,512]{2,1,0:T(8,128)(2,1)} %fac_any.1), custom_call_target="tpu_custom_call" | custom-call | tf_op jit(solution)/shard_map/pallas_call | solution.py:300
  41.2 1.4 %copy.9 = f32[16,512]{1,0:T(8,128)} copy(f32[16,512]{1,0:T(8,128)} %shard_map.73) | data formatting | bytes 65536
